TPU v7x, 128 devices: a whole 4x4x4 slice. The times are simulated.
128 devices in a mesh: gx: 16 (over y, z), gy: 8 (over x, core).
Axes of the slice: x: 4, y: 4, z: 4, core: 2. Of those that a mesh axis runs over, the one named last changes fastest.
Arguments:
- raw: bfloat16 [8, 128, 1024], P('gy', None, 'gx'), may hold values from -6 to 6
- section_order: int32 [8], replicated, may hold values from 0 to 7, each once
- margins: int32 [16, 8], replicated, may hold values from 1 to 4, as said below
- w_in: bfloat16 [28, 9], replicated, may hold values from -2 to 2
- b_in: float32 [28], replicated, may hold values from -3 to 3
- w_a: bfloat16 [27, 28, 28], replicated, may hold values from -0.21875 to 0.21875
- b_a: float32 [28], replicated, may hold values from -3 to 3
- w_d: bfloat16 [9, 36, 28], replicated, may hold values from -0.375 to 0.375
- b_d: float32 [36], replicated, may hold values from -3 to 3
- w_u: bfloat16 [28, 36], replicated, may hold values from -1 to 1
- w_o: bfloat16 [3, 28], replicated, may hold values from -1 to 1
- b_o: float32 [3], replicated, may hold values from -3 to 3
Outputs:
- affinities: float32 [3, 8, 128, 1024], P(None, None, 'gx', 'gy')
Inputs may be any that keep to these rules, and one draw needn't show every extreme that they name: `section_order`: each section is named once. margins of the groups; one group has margin 4 in every draw.
All inputs are finite; a program needn't handle non-finite values.
Results may differ from a plain program's by a relative error of at most 0.0065.
Values may be sent and summed in bfloat16 or wider, within the bound.
A program may use at most 128 MiB of HBM per device.

v0:
```python
import functools

import jax
import jax.numpy as jnp
import ml_dtypes
import numpy as np
from jax import lax
from jax.experimental import pallas as pl
from jax.experimental.pallas import tpu as pltpu
from jax.sharding import PartitionSpec as P

MESH = pl.DeviceIdType.MESH
F32 = jnp.float32
BF16 = jnp.bfloat16
BIG = -1e30


def iota(shape, dim):
    return lax.broadcasted_iota(jnp.int32, shape, dim)


def within(x, low, high):
    return (x >= low) & (x <= high)


def dot(a, b):
    return jnp.dot(a, b, preferred_element_type=F32)


def neighbours(gi):
    odd = lax.rem(gi, 2)
    column = lax.div(gi, 2)
    beside = lax.rem(column + 7 + 2 * odd, 8)
    return odd, column, beside


def unit_row(dx, block, channel):
    if dx == 1:
        return 32 * block + channel
    unit = 3 * (dx // 2) + block
    if unit < 5:
        return 96 + 28 * unit + channel
    return 236 + channel if channel < 20 else 8 + channel if channel < 24 else 36 + channel


def units_table():
    table = np.zeros((3, 3, 32, 256), np.float32)
    for block in range(3):
        for dx in range(3):
            for channel in range(28):
                table[block, dx, channel, unit_row(dx, block, channel)] = 1
    return table.reshape(288, 256).astype(ml_dtypes.bfloat16)


def level_table():
    spread = np.zeros((256, 256), np.float32)
    core = np.zeros((2, 128, 256), np.float32)
    side = np.zeros((2, 128, 512), np.float32)
    spread_side = np.zeros((2, 128, 128), np.float32)
    for lane in range(256):
        spread[lane // 2, lane] = spread[128 + lane // 2, lane] = 1
    for m in range(64):
        for fine in (0, 1):
            if m >= 1:
                core[:, 2 * m - 2 + fine, m] = 0.25
            if m <= 62:
                core[:, 2 * m + 2 + fine, 64 + m] = 0.25
            core[:, 2 * m + fine, 128 + m] = 0.25
    for section in range(8):
        for fine in (0, 1):
            for dx in range(3):
                for m in (0, 1):
                    left, right = m + dx - 1, 62 + m + dx - 1
                    if left <= 1:
                        side[:, 16 * section + 2 + 2 * left + fine, 128 * dx + 8 * section + 1 + m] = 0.25
                    if right >= 62:
                        side[:, 16 * section + 2 * right - 114 + fine, 128 * dx + 8 * section + 4 + m] = 0.25
            at = 384 + 64 * (section % 2) + section // 2
            side[:, 16 * section + fine, at] = 0.25
            side[:, 16 * section + 14 + fine, at + 60] = 0.25
        for x in range(4):
            spread_side[:, 8 * section + 1 + x // 2, 16 * section + 2 + x] = 1
            spread_side[:, 8 * section + 4 + x // 2, 16 * section + 10 + x] = 1
    parts = [spread, core.reshape(256, 256), side.reshape(256, 512), spread_side.reshape(256, 128)]
    return np.concatenate(parts, axis=1).astype(ml_dtypes.bfloat16)


def as_column(row, size):
    shape = (size, row.shape[1])
    return jnp.sum(jnp.where(iota(shape, 0) == iota(shape, 1), row, 0.0), axis=1, keepdims=True)


def tiled_taps(pad_ref, first, taps):
    tiles = []
    for start in range(0, taps, 4):
        tile = None
        for q in range(min(4, taps - start)):
            part = pad_ref[first + start + q].astype(F32)
            part = part if q == 0 else pltpu.roll(part, 32 * q, 1)
            tile = part if tile is None else tile + part
        tiles.append(tile)
    return jnp.concatenate(tiles, axis=1)


def lay_out_weights(
    units_ref,
    w_in_ref,
    b_in_ref,
    w_a_ref,
    b_a_ref,
    w_d_ref,
    b_d_ref,
    w_u_ref,
    w_o_ref,
    b_o_ref,
    pad_ref,
    conv_in_ref,
    conv_a_ref,
    conv_d_ref,
    w_q_ref,
    w_s_ref,
    bias_ref,
):
    pad_ref[...] = jnp.zeros_like(pad_ref)
    pad_ref[0, 0:9, 0:28] = w_in_ref[...]
    tap = iota((32, 128), 0)
    lane = iota((32, 128), 1)
    put = (lane == 16 * (tap % 3) + tap // 3) & (tap < 9)
    base = lax.dot_general(
        pad_ref[0],
        put.astype(F32).astype(BF16),
        (((0,), (0,)), ((), ())),
        preferred_element_type=F32,
    )[0:32]
    rest = as_column(b_in_ref[...], 32)
    flagged = jnp.zeros((32, 128), F32)
    for n in range(3):
        part = rest.astype(BF16).astype(F32)
        flagged = flagged + jnp.where(lane == 80 + n, part, 0.0)
        rest = rest - part
    stack = []
    for block in range(3):
        for dx in range(3):
            row = []
            for tile in range(5):
                y = 3 * tile + block
                if y > 13:
                    row.append(jnp.zeros((32, 128), F32))
                    continue
                moved = base if dx == y == 0 else pltpu.roll(base, 16 * dx + y, 1)
                off = (lane == 83 + dx) | ((lane == 86) & (y < 3)) | ((lane == 87) & (y >= 11))
                row.append(moved + flagged + jnp.where(off, BIG, 0.0))
            stack.append(jnp.concatenate(row, axis=1))
    made = lax.dot_general(
        units_ref[...],
        jnp.concatenate(stack, axis=0).astype(BF16),
        (((0,), (0,)), ((), ())),
        preferred_element_type=F32,
    ).astype(BF16)
    for tile in range(5):
        conv_in_ref[256 * tile : 256 * tile + 256] = made[:, 128 * tile : 128 * tile + 128]

    pad_ref[0] = jnp.zeros((32, 128), BF16)
    pad_ref[0:27, 0:28, 0:28] = w_a_ref[...]
    lane = iota((32, 384), 1)
    parts = [[] for _ in range(7)]
    for dz in range(3):
        taps = tiled_taps(pad_ref, 9 * dz, 9)
        for n, shift in enumerate((-1, -2, -1, 0, 1, 2, 0)):
            moved = taps if shift == 0 else pltpu.roll(taps, 96 * shift % 384, 1)
            low, high = 96 * max(shift, 0), 96 * min(3 + shift, 3)
            if n == 0:
                high = 96
            if n == 6:
                low = 96
            parts[n].append(jnp.where((lane >= low) & (lane < high), moved, 0.0))
    taps = jnp.concatenate([part for shift in parts for part in shift], axis=0).astype(BF16)
    conv_a_ref[...] = dot(taps[:, 0:288], units_ref[...]).astype(BF16)

    pad_ref[0:9] = jnp.zeros((9, 32, 128), BF16)
    pad_ref[0:9, 0:28, 0:36] = w_d_ref[...]
    taps = pad_ref[0:12].astype(F32).reshape(384, 128)
    taps = jnp.where(iota((384, 128), 0) < 288, taps, 0.0)
    taps = jnp.concatenate([taps[128 * n : 128 * n + 128].T[0:40] for n in range(3)], axis=1)
    taps = jnp.concatenate([taps, jnp.zeros((40, 384), F32)], axis=1)
    lane = iota((40, 768), 1)

    def spaced(*moves):
        total = None
        for first, dy, count in moves:
            by = 96 * (first - dy) % 768
            moved = taps if by == 0 else pltpu.roll(taps, by, 1)
            moved = jnp.where(within(lane, 96 * first, 96 * (first + count) - 1), moved, 0.0)
            total = moved if total is None else total + moved
        return total

    outs = [
        spaced((0, 0, 2), (6, 2, 1)),
        spaced((1, 0, 1), (6, 1, 1)),
        spaced((0, 0, 3)),
        spaced((1, 0, 3)),
        spaced((2, 0, 3)),
        spaced((3, 0, 3)),
        spaced((4, 2, 1), (7, 1, 1)),
        spaced((4, 1, 2), (7, 0, 1)),
    ]
    none = [jnp.zeros((8, 256), F32)]
    for at, tile, which in (
        (0, 0, (0, 1, 2, 3, 4)),
        (208, 1, (2, 3, 4, 5, 6, 7)),
        (448, 2, (0, 1, 5, 6, 7)),
    ):
        part = [outs[n][:, 256 * tile : 256 * tile + 256] for n in which]
        part = jnp.concatenate(part if tile == 1 else part + none, axis=0)
        conv_d_ref[at : at + part.shape[0]] = part.astype(BF16)

    w_o = w_o_ref[...].astype(F32)
    w_o = jnp.concatenate([jnp.broadcast_to(w_o[o : o + 1], (8, 28)) for o in range(3)], axis=0)
    w_o = jnp.concatenate([w_o, jnp.zeros((24, 4), F32)], axis=1)
    pad_ref[0] = jnp.zeros((32, 128), BF16)
    pad_ref[0, 0:28, 0:36] = w_u_ref[...]
    w_u = pad_ref[0].astype(F32)
    w_u = jnp.concatenate([w_u, jnp.zeros_like(w_u)], axis=1)
    w_u = w_u + pltpu.roll(w_u, 40, 1)
    w_u = w_u + pltpu.roll(w_u, 80, 1)
    w_q = dot(w_o.astype(BF16), w_u.astype(BF16))
    lane = iota((24, 256), 1)
    w_q = jnp.where(lane // 40 == (iota((24, 256), 0) % 8) // 2, w_q, 0.0)
    high = w_q.astype(BF16).astype(F32)
    w_q_ref[...] = jnp.concatenate([high, w_q - high], axis=0).astype(BF16)
    w_o = jnp.concatenate([w_o] * 12, axis=1)
    w_o = jnp.concatenate([w_o, w_o], axis=0)
    lane = iota((48, 384), 1) // 32
    row = iota((48, 384), 0)
    block = jnp.where(row < 24, row % 8, jnp.where(within(row % 8, 3, 4), row % 8 + 5, row % 8))
    w_s_ref[...] = jnp.where(lane == block, w_o, 0.0).astype(BF16)

    bias_ref[0:32] = jnp.broadcast_to(as_column(b_a_ref[...], 32), (32, 128))
    bias_ref[32:72] = jnp.broadcast_to(as_column(b_d_ref[...], 40), (40, 128))
    row = iota((48, 3), 0) % 24 // 8
    b_o = jnp.sum(jnp.where(row == iota((48, 3), 1), b_o_ref[...], 0.0), axis=1, keepdims=True)
    bias_ref[72:120] = jnp.broadcast_to(b_o, (48, 128))
    bias_ref[120:128] = jnp.zeros((8, 128), F32)


def fold(core, beyond, z):
    lane = iota((8, 128), 1)
    left = jnp.where(lane < 4, pltpu.roll(beyond, (126 - 16 * z) % 128, 1), 0.0)
    right = jnp.where(lane >= 124, pltpu.roll(beyond, (114 - 16 * z) % 128, 1), 0.0)
    return core + left + right


def blend_weights(gi, gj, margins_ref, blend_ref):
    margins = margins_ref[...].astype(F32)
    places = margins.shape

    def margin(step_y, step_x):
        y, x = gi + step_y, gj + step_x
        here = (iota(places, 0) == x) & (iota(places, 1) == y)
        value = jnp.sum(jnp.where(here, margins, 0.0), keepdims=True)
        return value, (y >= 0) & (y < 16) & (x >= 0) & (x < 8)

    def ramp(distance, pair):
        return jnp.clip(1.0 - distance / (pair[0] + 1.0), 0.0, 1.0) * jnp.where(pair[1], 1.0, 0.0)

    y = iota((8, 128), 0)
    lane = iota((8, 128), 1)
    upper = y < 4
    off_y = jnp.where(upper, y + 1, 8 - y).astype(F32)
    nth = lane % 16
    left = nth < 8
    off_x = jnp.where(
        within(nth, 2, 5), nth - 1, jnp.where(within(nth, 10, 13), 14 - nth, 99)
    ).astype(F32)
    m = {(a, b): margin(a, b) for a in (-1, 0, 1) for b in (-1, 0, 1) if (a, b) != (0, 0)}
    weight_y = jnp.where(upper, ramp(off_y, m[-1, 0]), ramp(off_y, m[1, 0]))
    weight_x = jnp.where(left, ramp(off_x, m[0, -1]), ramp(off_x, m[0, 1]))

    def corner(a, b):
        return ramp(off_y, m[a, b]) * ramp(off_x, m[a, b])

    weight_xy = jnp.where(
        upper,
        jnp.where(left, corner(-1, -1), corner(-1, 1)),
        jnp.where(left, corner(1, -1), corner(1, 1)),
    )
    blend_ref[0:8] = weight_y
    blend_ref[8:16] = weight_x
    blend_ref[16:24] = weight_xy
    blend_ref[24:32] = 1.0 / fold(1.0 + weight_y, weight_x + weight_xy, 0)


def flag_rows(gi, gj, side):
    kind = iota((16, 128), 0)
    lane = iota((16, 128), 1)
    dx = kind - 3
    if side:
        nth = lane % 16
        column = jnp.where(nth < 8, nth - 3 + dx, 113 + nth + dx)
        outside = column == jnp.where(nth < 8, 4, 123)
    else:
        column = lane + dx - 1
        outside = lane < 0
    outside = outside | ((column < 0) & (gj == 0)) | ((column > 127) & (gj == 7))
    value = (kind < 3) | (within(kind, 3, 5) & outside)
    value = value | ((kind == 6) & (gi == 0)) | ((kind == 7) & (gi == 15))
    return jnp.where(value, 1.0, 0.0).astype(BF16)


def shift_raw(order_ref, got_ref, got_edge_ref, taps_ref):
    lane = iota((8, 128), 1)
    tile = iota((16, 128), 1)
    sides = [jnp.zeros((16, 128), F32) for _ in range(5)]
    for z in range(8):
        slab = jnp.int32(0)
        for k in range(8):
            slab = jnp.maximum(slab, jnp.where(order_ref[k] == z, k, 0))
        near, far = [got_ref[n, slab].astype(F32) for n in range(2)]
        before, after = [jnp.broadcast_to(got_edge_ref[n, slab], (8, 128)) for n in range(2)]
        core = jnp.concatenate(
            [
                jnp.where(lane < 64, near, pltpu.roll(far, 64, 1)),
                jnp.where(lane < 64, pltpu.roll(near, 64, 1), far),
            ],
            axis=0,
        )
        before = jnp.concatenate(
            [pltpu.roll(before, n, 1, stride=16, stride_axis=0) for n in (6, 2)], axis=0
        )
        after = jnp.concatenate(
            [pltpu.roll(after, n, 1, stride=16, stride_axis=0) for n in (14, 10)], axis=0
        )
        low = jnp.where(tile < 6, pltpu.roll(core, 6, 1), after)
        high = jnp.where(tile >= 122, pltpu.roll(core, 122, 1), before)
        beside = jnp.where(tile < 64, low, high)
        for n in range(5):
            s = n - 2
            moved = core if s == 0 else pltpu.roll(core, -s % 128, 1)
            if s > 0:
                moved = jnp.where(tile >= 128 - s, pltpu.roll(beside, 122 - s, 1), moved)
            if s < 0:
                moved = jnp.where(tile < -s, pltpu.roll(beside, 6 - s, 1), moved)
            taps_ref[16 * n : 16 * n + 16, 128 * z : 128 * z + 128] = moved.astype(BF16)
            moved = pltpu.roll(beside, (16 * z + 8 - s) % 128, 1)
            sides[n] = jnp.where(tile // 16 == z, moved, sides[n])
    for n in range(5):
        taps_ref[16 * n : 16 * n + 16, 1024:1152] = sides[n].astype(BF16)


def exchange_kernel(*refs):
    hbm, refs = refs[0:14], refs[14:]
    taps_ref, made, blend_ref, table_ref, refs = refs[0], refs[1:7], refs[7], refs[8], refs[9:]
    loaded, refs = refs[0:13], refs[13:]
    pad_ref, send_ref, send_edge_ref, got_ref, got_edge_ref, load_sem, send_sem, recv_sem = refs
    raw_ref, order_ref, margins_ref, weights = loaded[0], loaded[1], loaded[2], loaded[3:]
    gi = lax.axis_index("gx")
    gj = lax.axis_index("gy")
    odd, column, beside = neighbours(gi)
    inner = (gi > 0) & (gi < 15)
    loads = [
        pltpu.make_async_copy(source, place, load_sem.at[n])
        for n, (source, place) in enumerate(zip(hbm, loaded + (table_ref,)))
    ]
    loads[0].start()
    barrier = pltpu.get_barrier_semaphore()

    for slab in range(8):
        for strip in (2 * gj, 2 * gj + 1):
            pl.semaphore_signal(barrier, inc=1, device_id=(strip, slab), device_id_type=MESH)

    @pl.when(gj > 0)
    def _():
        for slab in range(8):
            peer = (2 * gj - 1, slab)
            pl.semaphore_signal(barrier, inc=1, device_id=peer, device_id_type=MESH)

    @pl.when(gj < 7)
    def _():
        for slab in range(8):
            peer = (2 * gj + 2, slab)
            pl.semaphore_signal(barrier, inc=1, device_id=peer, device_id_type=MESH)
    for load in loads[1:]:
        load.start()

    lane = iota((128, 256), 1)
    wanted = iota((128, 256), 0) + jnp.where(lane < 128, -4, 4)
    rows = (wanted == lane % 128).astype(F32).astype(BF16)
    lane = iota((128, 128), 1)
    nth = lane % 16 - 8 * (1 - odd)
    cols = jnp.where(within(nth, 0, 3), nth, jnp.where(within(nth, 4, 7), nth + 60, -99)) + 60 * odd
    cols = (iota((128, 128), 0) == cols).astype(F32).astype(BF16)
    own = lane // 16 == 7 - iota((128, 128), 0) % 8
    gather = (iota((16, 128), 0) == iota((16, 128), 1) // 8).astype(F32).astype(BF16)
    loads[0].wait()
    raw = raw_ref[0].astype(F32)
    none = jnp.zeros_like(raw)
    raw = jnp.concatenate(
        [jnp.concatenate([raw, none], axis=1), jnp.concatenate([none, raw], axis=1)], axis=0
    ).astype(BF16)
    message = lax.dot_general(
        rows, raw, (((1,), (1,)), ((), ())), preferred_element_type=F32
    ).astype(BF16)
    send_ref[...] = message.reshape(16, 8, 128)
    edge = dot(gather, jnp.where(own, dot(message, cols), 0.0).astype(BF16))
    for row in range(16):
        send_edge_ref[row] = edge[row : row + 1]

    @pl.when(inner)
    def _():
        pl.semaphore_wait(barrier, 32)

    @pl.when(jnp.logical_not(inner))
    def _():
        pl.semaphore_wait(barrier, 16)

    for row in ROWS:
        for kind, source, target, place, wanted in (
            (0, send_ref.at[row], got_ref.at[odd, gj], column, True),
            (1, send_edge_ref.at[row], got_edge_ref.at[1 - odd, gj], beside, inner),
        ):
            here = (gi == row) & (gj == place)

            @pl.when(jnp.logical_not(here) & wanted)
            def _():
                pltpu.make_async_remote_copy(
                    src_ref=source,
                    dst_ref=target,
                    send_sem=send_sem.at[kind],
                    recv_sem=recv_sem.at[kind],
                    device_id=(row, place),
                    device_id_type=MESH,
                ).start()

            @pl.when(here & wanted)
            def _():
                pltpu.make_async_copy(source, target, recv_sem.at[kind]).start()

    for load in loads[1:]:
        load.wait()
    lay_out_weights(*weights, pad_ref, *made)
    blend_weights(gi, gj, margins_ref, blend_ref)
    flags = flag_rows(gi, gj, False)
    for z in range(8):
        taps_ref[80:96, 128 * z : 128 * z + 128] = flags
    taps_ref[80:96, 1024:1152] = flag_rows(gi, gj, True)


    def got(ref, kind):
        pltpu.make_async_copy(ref, ref, recv_sem.at[kind]).wait()

    got(got_ref, 0)

    @pl.when(within(gj, 1, 6))
    def _():
        got(got_edge_ref, 1)

    @pl.when(gj == 0)
    def _():
        got(got_edge_ref.at[1], 1)
        got_edge_ref[0] = jnp.zeros((8, 1, 128), F32)

    @pl.when(gj == 7)
    def _():
        got(got_edge_ref.at[0], 1)
        got_edge_ref[1] = jnp.zeros((8, 1, 128), F32)

    shift_raw(order_ref, got_ref, got_edge_ref, taps_ref)

    def sent(ref, count):
        kind = 0 if ref is send_ref else 1
        ref = ref.at[0:count]
        pltpu.make_async_copy(ref, ref, send_sem.at[kind]).wait()

    @pl.when(gj == column)
    def _():
        sent(send_ref, 15)

    @pl.when(gj != column)
    def _():
        sent(send_ref, 16)

    @pl.when(inner & (gj == beside))
    def _():
        sent(send_edge_ref, 15)

    @pl.when(inner & (gj != beside))
    def _():
        sent(send_edge_ref, 16)


ROWS = (0, 1, 3, 4, 12, 2, 5, 7, 8, 13, 15, 6, 9, 11, 14, 10)


TAPS = jax.ShapeDtypeStruct((96, 1152), BF16)
MADE = (
    jax.ShapeDtypeStruct((1280, 128), BF16),
    jax.ShapeDtypeStruct((672, 256), BF16),
    jax.ShapeDtypeStruct((656, 256), BF16),
    jax.ShapeDtypeStruct((48, 256), BF16),
    jax.ShapeDtypeStruct((48, 384), BF16),
    jax.ShapeDtypeStruct((128, 128), F32),
)
BLEND = jax.ShapeDtypeStruct((32, 128), F32)
TABLE = jax.ShapeDtypeStruct((256, 1152), BF16)


def as_they_lie(raw, section_order, margins, w_in, b_in, w_a, b_a, w_d, b_d, w_u, w_o, b_o):
    return (
        jnp.transpose(raw, (0, 2, 1)),
        section_order,
        margins.T,
        jnp.asarray(units_table()),
        w_in.T,
        b_in[None],
        w_a,
        b_a[None],
        jnp.transpose(w_d, (0, 2, 1)),
        b_d[None],
        w_u,
        w_o,
        b_o[None],
        jnp.asarray(level_table()),
    )


def exchange(*arrays):
    arrays = [pltpu.with_memory_space_constraint(x, pltpu.HBM) for x in as_they_lie(*arrays)]
    vmem = pl.BlockSpec(memory_space=pltpu.VMEM)
    places = [pltpu.SMEM if n == 1 else pltpu.VMEM for n in range(13)]
    return pl.pallas_call(
        exchange_kernel,
        out_shape=(TAPS,) + MADE + (BLEND, TABLE),
        in_specs=[pl.BlockSpec(memory_space=pltpu.HBM)] * 14,
        out_specs=(vmem,) * 9,
        scratch_shapes=[place(x.shape, x.dtype) for place, x in zip(places, arrays)]
        + [
            pltpu.VMEM((27, 32, 128), BF16),
            pltpu.VMEM((16, 8, 128), BF16),
            pltpu.VMEM((16, 1, 128), F32),
            pltpu.VMEM((2, 8, 8, 128), BF16),
            pltpu.VMEM((2, 8, 1, 128), F32),
            pltpu.SemaphoreType.DMA((14,)),
            pltpu.SemaphoreType.DMA((2,)),
            pltpu.SemaphoreType.DMA((2,)),
        ],
        compiler_params=pltpu.CompilerParams(
            collective_id=0, has_side_effects=True, vmem_limit_bytes=12 * 1024 * 1024
        ),
    )(*arrays)


def network_kernel(
    taps_ref,
    conv_in_ref,
    conv_a_ref,
    conv_d_ref,
    w_q_ref,
    w_s_ref,
    bias_ref,
    blend_ref,
    table_ref,
    out_ref,
    h_ref,
    a_ref,
    d_ref,
    e_ref,
):
    bias_a = bias_ref[0:32]
    bias_d = jnp.concatenate([bias_ref[32:72]] * 8, axis=0)
    bias_o = bias_ref[72:120]
    weight_y, weight_x, weight_xy, scale = [blend_ref[8 * n : 8 * n + 8] for n in range(4)]
    margins = slice(1024, 1152)
    lane = iota((256, 128), 1)

    def pair(q):
        return slice(256 * q, 256 * q + 256)

    def section(z):
        return slice(128 * z, 128 * z + 128)

    def wide(column, at):
        return column if at.stop - at.start == 128 else jnp.concatenate([column, column], axis=1)

    def first_level(at):
        for tile in range(5):
            h = dot(conv_in_ref[256 * tile : 256 * tile + 256, 0:96], taps_ref[:, at])
            h_ref[tile, :, at] = jnp.maximum(h.astype(BF16), 0)

    places = (0, 1, 2, 3, 4, 5, 6, 7, 8, 9, 12, 13, 10, 11)

    def products(at):
        sums = [None] * 14
        width = at.stop - at.start
        for tile, first, rows in (
            (0, 3, (0, 1, 2)),
            (1, 1, (1, 2, 3, 4, 5)),
            (2, 0, (12, 4, 5, 6, 7, 8, 13)),
            (3, 1, (7, 8, 9, 10, 11)),
            (4, 1, (10, 11)),
        ):
            product = dot(conv_a_ref[96 * first : 96 * (first + len(rows))], h_ref[tile, :, at])
            product = product.reshape(len(rows), 3, 32, width)
            for n, row in enumerate(rows):
                part = product[n]
                sums[row] = part if sums[row] is None else sums[row] + part
                if tile == 1 and row == 5:
                    sums[12] = part
        return sums

    def finish(row, at, total):
        block = (row + 1 if row < 12 else row - 6) if row != 12 else 6
        tile, nth = block // 3, block % 3
        centre = h_ref[tile, 32 * nth : 32 * nth + 32, at].astype(F32)
        a_ref[places[row], :, at] = (centre + jnp.maximum(total + bias_a, 0.0)).astype(BF16)

    def pooled_rows(at):
        even = jnp.concatenate([a_ref[n, :, at] for n in (0, 2, 4, 6, 8, 12, 4, 11)], axis=0)
        late = jnp.concatenate([a_ref[n, :, at] for n in (1, 3, 5, 7, 9, 13, 10, 7)], axis=0)
        return jnp.concatenate([even, late], axis=1)

    def keep(dx, at, value):
        d_ref[:, dx, :, at] = value.astype(BF16).reshape(8, 32, 128)

    def pool(q, ends):
        both = jnp.concatenate([pooled_rows(section(2 * q)), pooled_rows(section(2 * q + 1))], axis=0)
        d = dot(both, table_ref[:, 256:512])
        one, two = d[0:256, 0:128], pltpu.roll(d[256:512, 0:128], 64, 1)
        low = lane < 64
        keep(1, section(q), jnp.where(low, d[0:256, 128:256], pltpu.roll(d[256:512, 128:256], 64, 1)))
        end = ends if q == 0 else pltpu.roll(ends, 128 - q, 1)
        keep(0, section(q), jnp.where(lane % 64 == 0, end, jnp.where(low, one, two)))
        end = ends if q == 3 else pltpu.roll(ends, 3 - q, 1)
        moved = pltpu.roll(jnp.where(low, two, one), 64, 1)
        keep(2, section(q), jnp.where(lane % 64 == 63, end, moved))

    def coarse(at):
        d = d_ref[:, :, :, at].reshape(768, at.stop - at.start)
        one = dot(conv_d_ref[0:208], d[0:256])
        two = dot(conv_d_ref[208:448], d[256:512])
        three = dot(conv_d_ref[448:656], d[512:768])
        e = jnp.concatenate(
            [
                one[0:80] + three[0:80],
                one[80:200] + two[0:120],
                two[120:240] + three[80:200],
            ],
            axis=0,
        )
        e_ref[:, at] = jnp.maximum(e + wide(bias_d, at), 0.0).astype(BF16)

    def lifted(at, table):
        own = dot(w_q_ref[:, 0:160], e_ref[80:240, at])
        other = dot(w_q_ref[:, 0:160], jnp.concatenate([e_ref[0:80, at], e_ref[240:320, at]], axis=0))
        q = jnp.concatenate([own[0:24] + own[24:48], other[0:24] + other[24:48]], axis=0)
        high = q.astype(BF16).astype(F32)
        return dot(jnp.concatenate([high, q - high], axis=1).astype(BF16), table)

    def chances(at, up):
        s = dot(w_s_ref[:, 0:320], a_ref[2:12, :, at].reshape(320, at.stop - at.start))
        return jax.nn.sigmoid(s + up + wide(bias_o, at))

    def head(q, beyond):
        s = chances(pair(q), lifted(section(q), table_ref[:, 0:256]))
        for half in range(2):
            for o in range(3):
                own = s[8 * o : 8 * o + 8, 128 * half : 128 * half + 128]
                other = s[24 + 8 * o : 32 + 8 * o, 128 * half : 128 * half + 128]
                z = 2 * q + half
                out_ref[o, z] = fold(own + other * weight_y, beyond[o], z) * scale

    first_level(margins)
    first_level(pair(0))
    sums = products(margins)
    along = iota((32, 128), 1)
    for row in range(14):
        before, here, after = sums[row][0], sums[row][1], sums[row][2]
        before = jnp.where(along >= 16, pltpu.roll(before, 16, 1), 0.0)
        after = jnp.where(along < 112, pltpu.roll(after, 112, 1), 0.0)
        finish(row, margins, here + before + after)
    first_level(pair(1))
    previous = products(pair(0))
    d = dot(pooled_rows(margins), table_ref[:, 512:1024])
    ends = d[:, 384:512]
    for dx in range(3):
        keep(dx, slice(512, 640), d[:, 128 * dx : 128 * dx + 128])
    current = None
    beyond = None
    older = None
    for q in range(4):
        current = products(pair(q + 1)) if q < 3 else None
        for row in range(14):
            p = previous[row]
            total = p[1, :, 0:128] + p[2, :, 128:256]
            if q > 0:
                total = total + older[row][0, :, 128:256]
            finish(row, section(2 * q), total)
            total = p[1, :, 128:256] + p[0, :, 0:128]
            if q < 3:
                total = total + current[row][2, :, 0:128]
            finish(row, section(2 * q + 1), total)
        older, previous = previous, current
        if q < 2:
            first_level(pair(q + 2))
        if q == 0:
            coarse(slice(512, 640))
            beyond = chances(margins, lifted(slice(512, 640), table_ref[:, 1024:1152]))
            beyond = [
                beyond[8 * o : 8 * o + 8] * weight_x + beyond[24 + 8 * o : 32 + 8 * o] * weight_xy
                for o in range(3)
            ]
        pool(q, ends)
        if q % 2 == 1:
            coarse(slice(128 * q - 128, 128 * q + 128))
            head(q - 1, beyond)
            head(q, beyond)


def network(*made, **options):
    vmem = pl.BlockSpec(memory_space=pltpu.VMEM)
    return pl.pallas_call(
        network_kernel,
        out_shape=jax.ShapeDtypeStruct((3, 8, 8, 128), F32),
        in_specs=[vmem] * 9,
        out_specs=vmem,
        scratch_shapes=[
            pltpu.VMEM((5, 256, 1152), BF16),
            pltpu.VMEM((14, 32, 1152), BF16),
            pltpu.VMEM((8, 3, 32, 640), BF16),
            pltpu.VMEM((320, 640), BF16),
        ],
        compiler_params=pltpu.CompilerParams(vmem_limit_bytes=32 * 1024 * 1024),
        **options,
    )(*made)


def per_device(*arrays):
    return network(*exchange(*arrays))


def solution(mesh):
    placed = (P("gy", None, "gx"), P(), P(), P(), P(), P(), P(), P(), P(), P(), P(), P())
    return jax.shard_map(
        per_device, mesh=mesh, in_specs=placed, out_specs=P(None, None, "gx", "gy"), check_vma=False
    )
```

profile of v0, /device:TPU:1, one launch (start us, length us, event | category | flops | bytes accessed | tf_op | source)
XLA Modules:
  0.0 20.0 jit_solution(9729168980699944810)
XLA Ops:
  0.0 13.9 %shard_map.136 = (bf16[96,1152]{1,0:T(8,128)(2,1)S(1)}, bf16[1280,128]{1,0:T(8,128)(2,1)S(1)}, bf16[672,256]{1,0:T(8,128)(2,1)S(1)}, bf16[656,256]{1,0:T(8,128)(...) custom-call(bf16[1,64,128]{2,1,0:T(8,128)(2,1)} %bitcast.9, ...), custom_call_target="tpu_custom_call" | custom-call | tf_op jit(solution)/shard_map/pallas_call | solution.py:530
  13.9 6.1 %shard_map.137 = f32[3,8,8,128]{3,2,1,0:T(8,128)} custom-call(bf16[96,1152]{1,0:T(8,128)(2,1)S(1)} %get-tuple-element.14.taps_ref, bf16[1280,128]{1,0:T(8,128)(2,1)S(1)} %get-tuple-element.15.conv_in_ref, bf16[672,256]{1,0:T(8,128)(2,1)S(1)} %get-tuple-element.16.conv_a_ref, bf16[656,256]{1,0:T(8,128)(2,1)S(1)} %get-tuple-element.17.conv_d_ref, ...), custom_call_target="tpu_custom_call" | custom-call | tf_op jit(solution)/shard_map/pallas_call | solution.py:720
where the time goes:
time: 20.2 us; the launch traced here: 20 us
  Pallas kernels  20 us (99%)
    pallas_call x1, Pallas kernels, exchange(): pl.pallas_call(exchange_kernel, out_shape=(TAPS,) + MADE + (BLEND, TABLE)...  13.9 us
    pallas_call x1, Pallas kernels, network(): pl.pallas_call(network_kernel, out_shape=jax.ShapeDtypeStruct((3, 8, 8, 1...  6.09 us

commit v1 on v0

--- a/solution.py
+++ b/solution.py
@@ -351,7 +351,7 @@
     hbm, refs = refs[0:14], refs[14:]
     taps_ref, made, blend_ref, table_ref, refs = refs[0], refs[1:7], refs[7], refs[8], refs[9:]
     loaded, refs = refs[0:13], refs[13:]
-    pad_ref, send_ref, send_edge_ref, got_ref, got_edge_ref, load_sem, send_sem, recv_sem = refs
+    pad_ref, send_ref, send_edge_ref, got_ref, got_edge_ref, load_sem, send_sem, recv_sem, mate_sem = refs
     raw_ref, order_ref, margins_ref, weights = loaded[0], loaded[1], loaded[2], loaded[3:]
     gi = lax.axis_index("gx")
     gj = lax.axis_index("gy")
@@ -364,21 +364,33 @@
     loads[0].start()
     barrier = pltpu.get_barrier_semaphore()
 
-    for slab in range(8):
+    core = lax.rem(gj, 2)
+    mate = (gi, gj + 1 - 2 * core)
+    group = jnp.int32(1)
+    for row in SOON:
+        group = jnp.where(gi == row, 0, group)
+
+    @pl.when(core == 1)
+    def _():
+        pl.semaphore_signal(barrier, inc=1, device_id=mate, device_id_type=MESH)
+
+    for chip in range(4):
         for strip in (2 * gj, 2 * gj + 1):
-            pl.semaphore_signal(barrier, inc=1, device_id=(strip, slab), device_id_type=MESH)
+            peer = (strip, 2 * chip + group)
+            pl.semaphore_signal(barrier, inc=1, device_id=peer, device_id_type=MESH)
 
     @pl.when(gj > 0)
     def _():
-        for slab in range(8):
-            peer = (2 * gj - 1, slab)
+        for chip in range(4):
+            peer = (2 * gj - 1, 2 * chip + group)
             pl.semaphore_signal(barrier, inc=1, device_id=peer, device_id_type=MESH)
 
     @pl.when(gj < 7)
     def _():
-        for slab in range(8):
-            peer = (2 * gj + 2, slab)
+        for chip in range(4):
+            peer = (2 * gj + 2, 2 * chip + group)
             pl.semaphore_signal(barrier, inc=1, device_id=peer, device_id_type=MESH)
+
     for load in loads[1:]:
         load.start()
 
@@ -405,15 +417,19 @@
     for row in range(16):
         send_edge_ref[row] = edge[row : row + 1]
 
-    @pl.when(inner)
-    def _():
-        pl.semaphore_wait(barrier, 32)
-
-    @pl.when(jnp.logical_not(inner))
-    def _():
-        pl.semaphore_wait(barrier, 16)
-
-    for row in ROWS:
+    soon = jnp.where(inner, 2 * len(SOON), len(SOON))
+    late = jnp.where(inner, 2 * len(LATE), len(LATE))
+
+    @pl.when(core == 0)
+    def _():
+        pl.semaphore_wait(barrier, soon + 1)
+        pl.semaphore_signal(mate_sem, inc=1, device_id=mate, device_id_type=MESH)
+
+    @pl.when(core == 1)
+    def _():
+        pl.semaphore_wait(mate_sem, 1)
+
+    def send(row):
         for kind, source, target, place, wanted in (
             (0, send_ref.at[row], got_ref.at[odd, gj], column, True),
             (1, send_edge_ref.at[row], got_edge_ref.at[1 - odd, gj], beside, inner),
@@ -435,6 +451,9 @@
             def _():
                 pltpu.make_async_copy(source, target, recv_sem.at[kind]).start()
 
+    for row in SOON:
+        send(row)
+
     for load in loads[1:]:
         load.wait()
     lay_out_weights(*weights, pad_ref, *made)
@@ -444,6 +463,17 @@
         taps_ref[80:96, 128 * z : 128 * z + 128] = flags
     taps_ref[80:96, 1024:1152] = flag_rows(gi, gj, True)
 
+    @pl.when(core == 0)
+    def _():
+        pl.semaphore_wait(mate_sem, 1)
+
+    @pl.when(core == 1)
+    def _():
+        pl.semaphore_wait(barrier, late)
+        pl.semaphore_signal(mate_sem, inc=1, device_id=mate, device_id_type=MESH)
+
+    for row in LATE:
+        send(row)
 
     def got(ref, kind):
         pltpu.make_async_copy(ref, ref, recv_sem.at[kind]).wait()
@@ -488,7 +518,9 @@
         sent(send_edge_ref, 16)
 
 
-ROWS = (0, 1, 3, 4, 12, 2, 5, 7, 8, 13, 15, 6, 9, 11, 14, 10)
+ROWS = (0, 1, 4, 8, 12, 5, 2, 9, 13, 3, 6, 7, 10, 14, 11, 15)
+SOON = ROWS[:5]
+LATE = ROWS[5:]
 
 
 TAPS = jax.ShapeDtypeStruct((96, 1152), BF16)
@@ -542,6 +574,7 @@
             pltpu.SemaphoreType.DMA((14,)),
             pltpu.SemaphoreType.DMA((2,)),
             pltpu.SemaphoreType.DMA((2,)),
+            pltpu.SemaphoreType.REGULAR,
         ],
         compiler_params=pltpu.CompilerParams(
             collective_id=0, has_side_effects=True, vmem_limit_bytes=12 * 1024 * 1024

time: 20.2 us -> 18.1 us (0.90)
  Pallas kernels: 20 us -> 17.9 us
    pallas_call x1, Pallas kernels: 13.9 us -> 11.8 us  [exchange(): pl.pallas_call(exchange_kernel, out_shape=(TAPS,) + MADE + (BLEND, TABLE)...]
where the time goes in v1:
time: 18.1 us; the launch traced here: 17.9 us
  Pallas kernels  17.9 us (99%)
    pallas_call x1, Pallas kernels, exchange(): pl.pallas_call(exchange_kernel, out_shape=(TAPS,) + MADE + (BLEND, TABLE)...  11.8 us
    pallas_call x1, Pallas kernels, network(): pl.pallas_call(network_kernel, out_shape=jax.ShapeDtypeStruct((3, 8, 8, 1...  6.09 us

profile of v1, /device:TPU:1, one launch (start us, length us, event | category | flops | bytes accessed | tf_op | source)
XLA Modules:
  0.0 17.9 jit_solution(5742182624110577811)
XLA Ops:
  0.0 11.8 %shard_map.136 = (bf16[96,1152]{1,0:T(8,128)(2,1)S(1)}, bf16[1280,128]{1,0:T(8,128)(2,1)S(1)}, bf16[672,256]{1,0:T(8,128)(2,1)S(1)}, bf16[656,256]{1,0:T(8,128)(...) custom-call(bf16[1,64,128]{2,1,0:T(8,128)(2,1)} %bitcast.9, ...), custom_call_target="tpu_custom_call" | custom-call | tf_op jit(solution)/shard_map/pallas_call | solution.py:562
  11.8 6.1 %shard_map.137 = f32[3,8,8,128]{3,2,1,0:T(8,128)} custom-call(bf16[96,1152]{1,0:T(8,128)(2,1)S(1)} %get-tuple-element.14.taps_ref, bf16[1280,128]{1,0:T(8,128)(2,1)S(1)} %get-tuple-element.15.conv_in_ref, bf16[672,256]{1,0:T(8,128)(2,1)S(1)} %get-tuple-element.16.conv_a_ref, bf16[656,256]{1,0:T(8,128)(2,1)S(1)} %get-tuple-element.17.conv_d_ref, ...), custom_call_target="tpu_custom_call" | custom-call | tf_op jit(solution)/shard_map/pallas_call | solution.py:753

commit v2 on v1

--- a/solution.py
+++ b/solution.py
@@ -307,14 +307,12 @@
     return jnp.where(value, 1.0, 0.0).astype(BF16)
 
 
-def shift_raw(order_ref, got_ref, got_edge_ref, taps_ref):
+def shift_raw(slabs, got_ref, got_edge_ref, taps_ref):
     lane = iota((8, 128), 1)
     tile = iota((16, 128), 1)
     sides = [jnp.zeros((16, 128), F32) for _ in range(5)]
     for z in range(8):
-        slab = jnp.int32(0)
-        for k in range(8):
-            slab = jnp.maximum(slab, jnp.where(order_ref[k] == z, k, 0))
+        slab = slabs[z]
         near, far = [got_ref[n, slab].astype(F32) for n in range(2)]
         before, after = [jnp.broadcast_to(got_edge_ref[n, slab], (8, 128)) for n in range(2)]
         core = jnp.concatenate(
@@ -475,6 +473,13 @@
     for row in LATE:
         send(row)
 
+    slabs = []
+    for z in range(8):
+        slab = jnp.int32(0)
+        for k in range(8):
+            slab = jnp.maximum(slab, jnp.where(order_ref[k] == z, k, 0))
+        slabs.append(slab)
+
     def got(ref, kind):
         pltpu.make_async_copy(ref, ref, recv_sem.at[kind]).wait()
 
@@ -494,7 +499,7 @@
         got(got_edge_ref.at[0], 1)
         got_edge_ref[1] = jnp.zeros((8, 1, 128), F32)
 
-    shift_raw(order_ref, got_ref, got_edge_ref, taps_ref)
+    shift_raw(slabs, got_ref, got_edge_ref, taps_ref)
 
     def sent(ref, count):
         kind = 0 if ref is send_ref else 1
@@ -603,7 +608,6 @@
     bias_o = bias_ref[72:120]
     weight_y, weight_x, weight_xy, scale = [blend_ref[8 * n : 8 * n + 8] for n in range(4)]
     margins = slice(1024, 1152)
-    lane = iota((256, 128), 1)
 
     def pair(q):
         return slice(256 * q, 256 * q + 256)
@@ -615,30 +619,28 @@
         return column if at.stop - at.start == 128 else jnp.concatenate([column, column], axis=1)
 
     def first_level(at):
-        for tile in range(5):
-            h = dot(conv_in_ref[256 * tile : 256 * tile + 256, 0:96], taps_ref[:, at])
-            h_ref[tile, :, at] = jnp.maximum(h.astype(BF16), 0)
+        h = dot(conv_in_ref[:, 0:96], taps_ref[:, at]).astype(BF16)
+        h_ref[:, :, at] = jnp.maximum(h, 0).reshape(5, 256, at.stop - at.start)
 
     places = (0, 1, 2, 3, 4, 5, 6, 7, 8, 9, 12, 13, 10, 11)
 
-    def products(at):
-        sums = [None] * 14
-        width = at.stop - at.start
-        for tile, first, rows in (
-            (0, 3, (0, 1, 2)),
-            (1, 1, (1, 2, 3, 4, 5)),
-            (2, 0, (12, 4, 5, 6, 7, 8, 13)),
-            (3, 1, (7, 8, 9, 10, 11)),
-            (4, 1, (10, 11)),
-        ):
-            product = dot(conv_a_ref[96 * first : 96 * (first + len(rows))], h_ref[tile, :, at])
-            product = product.reshape(len(rows), 3, 32, width)
-            for n, row in enumerate(rows):
-                part = product[n]
-                sums[row] = part if sums[row] is None else sums[row] + part
-                if tile == 1 and row == 5:
-                    sums[12] = part
-        return sums
+    tiles = (
+        (3, (0, 1, 2), (0,)),
+        (1, (1, 2, 3, 4, 5), (1, 2, 3)),
+        (0, (12, 4, 5, 6, 7, 8, 13), (4, 5, 6, 12, 13)),
+        (1, (7, 8, 9, 10, 11), (7, 8, 9)),
+        (1, (10, 11), (10, 11)),
+    )
+
+    def products(tile, at, sums):
+        first, rows, _ = tiles[tile]
+        product = dot(conv_a_ref[96 * first : 96 * (first + len(rows))], h_ref[tile, :, at])
+        product = product.reshape(len(rows), 3, 32, at.stop - at.start)
+        for n, row in enumerate(rows):
+            part = product[n]
+            sums[row] = sums[row] + part if row in sums else part
+            if tile == 1 and row == 5:
+                sums[12] = part
 
     def finish(row, at, total):
         block = (row + 1 if row < 12 else row - 6) if row != 12 else 6
@@ -654,23 +656,36 @@
     def keep(dx, at, value):
         d_ref[:, dx, :, at] = value.astype(BF16).reshape(8, 32, 128)
 
-    def pool(q, ends):
+    def pool(q):
         both = jnp.concatenate([pooled_rows(section(2 * q)), pooled_rows(section(2 * q + 1))], axis=0)
-        d = dot(both, table_ref[:, 256:512])
-        one, two = d[0:256, 0:128], pltpu.roll(d[256:512, 0:128], 64, 1)
+        return dot(both, table_ref[:, 256:512])
+
+    def pooled(q, d, ends):
+        lane = iota((32, 128), 1)
         low = lane < 64
-        keep(1, section(q), jnp.where(low, d[0:256, 128:256], pltpu.roll(d[256:512, 128:256], 64, 1)))
-        end = ends if q == 0 else pltpu.roll(ends, 128 - q, 1)
-        keep(0, section(q), jnp.where(lane % 64 == 0, end, jnp.where(low, one, two)))
-        end = ends if q == 3 else pltpu.roll(ends, 3 - q, 1)
-        moved = pltpu.roll(jnp.where(low, two, one), 64, 1)
-        keep(2, section(q), jnp.where(lane % 64 == 63, end, moved))
+        for block in range(8):
+            rows, more = slice(32 * block, 32 * block + 32), slice(256 + 32 * block, 288 + 32 * block)
+            one, two = d[rows, 0:128], pltpu.roll(d[more, 0:128], 64, 1)
+            end = ends[rows]
+            before = end if q == 0 else pltpu.roll(end, 128 - q, 1)
+            after = end if q == 3 else pltpu.roll(end, 3 - q, 1)
+            moved = pltpu.roll(jnp.where(low, two, one), 64, 1)
+            for dx, value in (
+                (0, jnp.where(lane % 64 == 0, before, jnp.where(low, one, two))),
+                (1, jnp.where(low, d[rows, 128:256], pltpu.roll(d[more, 128:256], 64, 1))),
+                (2, jnp.where(lane % 64 == 63, after, moved)),
+            ):
+                d_ref[block, dx, :, section(q)] = value.astype(BF16)
 
     def coarse(at):
         d = d_ref[:, :, :, at].reshape(768, at.stop - at.start)
         one = dot(conv_d_ref[0:208], d[0:256])
         two = dot(conv_d_ref[208:448], d[256:512])
         three = dot(conv_d_ref[448:656], d[512:768])
+        return one, two, three
+
+    def coarsened(at, parts):
+        one, two, three = parts
         e = jnp.concatenate(
             [
                 one[0:80] + three[0:80],
@@ -681,19 +696,23 @@
         )
         e_ref[:, at] = jnp.maximum(e + wide(bias_d, at), 0.0).astype(BF16)
 
-    def lifted(at, table):
+    def lift(at):
         own = dot(w_q_ref[:, 0:160], e_ref[80:240, at])
         other = dot(w_q_ref[:, 0:160], jnp.concatenate([e_ref[0:80, at], e_ref[240:320, at]], axis=0))
+        return own, other
+
+    def spread(parts, table):
+        own, other = parts
         q = jnp.concatenate([own[0:24] + own[24:48], other[0:24] + other[24:48]], axis=0)
         high = q.astype(BF16).astype(F32)
         return dot(jnp.concatenate([high, q - high], axis=1).astype(BF16), table)
 
-    def chances(at, up):
+    def fine(at):
         s = dot(w_s_ref[:, 0:320], a_ref[2:12, :, at].reshape(320, at.stop - at.start))
-        return jax.nn.sigmoid(s + up + wide(bias_o, at))
-
-    def head(q, beyond):
-        s = chances(pair(q), lifted(section(q), table_ref[:, 0:256]))
+        return s + wide(bias_o, at)
+
+    def blend(q, s, beyond):
+        s = jax.nn.sigmoid(s)
         for half in range(2):
             for o in range(3):
                 own = s[8 * o : 8 * o + 8, 128 * half : 128 * half + 128]
@@ -703,49 +722,130 @@
 
     first_level(margins)
     first_level(pair(0))
-    sums = products(margins)
+    sums = {}
     along = iota((32, 128), 1)
-    for row in range(14):
-        before, here, after = sums[row][0], sums[row][1], sums[row][2]
-        before = jnp.where(along >= 16, pltpu.roll(before, 16, 1), 0.0)
-        after = jnp.where(along < 112, pltpu.roll(after, 112, 1), 0.0)
-        finish(row, margins, here + before + after)
+
+    def finish_margins(tile):
+        for row in tiles[tile][2]:
+            before, here, after = sums[row][0], sums[row][1], sums[row][2]
+            before = jnp.where(along >= 16, pltpu.roll(before, 16, 1), 0.0)
+            after = jnp.where(along < 112, pltpu.roll(after, 112, 1), 0.0)
+            finish(row, margins, here + before + after)
+
+    for tile in range(5):
+        products(tile, margins, sums)
+        if tile > 0:
+            finish_margins(tile - 1)
     first_level(pair(1))
-    previous = products(pair(0))
-    d = dot(pooled_rows(margins), table_ref[:, 512:1024])
-    ends = d[:, 384:512]
-    for dx in range(3):
-        keep(dx, slice(512, 640), d[:, 128 * dx : 128 * dx + 128])
-    current = None
-    beyond = None
-    older = None
-    for q in range(4):
-        current = products(pair(q + 1)) if q < 3 else None
-        for row in range(14):
-            p = previous[row]
-            total = p[1, :, 0:128] + p[2, :, 128:256]
+    finish_margins(4)
+
+    p = [{}, {}, {}, {}]
+
+    def finish_sections(q, tile):
+        for row in tiles[tile][2]:
+            here = p[q][row]
             if q > 0:
-                total = total + older[row][0, :, 128:256]
+                last = p[q - 1][row]
+                total = last[1, :, 128:256] + last[0, :, 0:128] + here[2, :, 0:128]
+                finish(row, section(2 * q - 1), total)
+            total = here[1, :, 0:128] + here[2, :, 128:256]
+            if q > 0:
+                total = total + p[q - 1][row][0, :, 128:256]
             finish(row, section(2 * q), total)
-            total = p[1, :, 128:256] + p[0, :, 0:128]
-            if q < 3:
-                total = total + current[row][2, :, 0:128]
-            finish(row, section(2 * q + 1), total)
-        older, previous = previous, current
-        if q < 2:
-            first_level(pair(q + 2))
-        if q == 0:
-            coarse(slice(512, 640))
-            beyond = chances(margins, lifted(slice(512, 640), table_ref[:, 1024:1152]))
-            beyond = [
-                beyond[8 * o : 8 * o + 8] * weight_x + beyond[24 + 8 * o : 32 + 8 * o] * weight_xy
-                for o in range(3)
-            ]
-        pool(q, ends)
-        if q % 2 == 1:
-            coarse(slice(128 * q - 128, 128 * q + 128))
-            head(q - 1, beyond)
-            head(q, beyond)
+            if q == 3:
+                finish(row, section(7), here[1, :, 128:256] + here[0, :, 0:128])
+
+    def residual(q, beside):
+        for tile in range(5):
+            products(tile, pair(q), p[q])
+            if tile > 0:
+                finish_sections(q, tile - 1)
+            for task in beside[tile : tile + 1]:
+                task()
+
+    got = {}
+
+    def margins_pool():
+        got["side"] = dot(pooled_rows(margins), table_ref[:, 512:1024])
+
+    def margins_pooled():
+        for dx in range(3):
+            keep(dx, slice(512, 640), got["side"][:, 128 * dx : 128 * dx + 128])
+        got["ends"] = got["side"][:, 384:512]
+
+    def margins_coarse():
+        got["e"] = coarse(slice(512, 640))
+        got["fine"] = fine(margins)
+
+    def margins_coarsened():
+        coarsened(slice(512, 640), got["e"])
+
+    def margins_lift():
+        got["q"] = lift(slice(512, 640))
+
+    def margins_spread():
+        got["up"] = spread(got["q"], table_ref[:, 1024:1152])
+
+    def margins_done():
+        s = jax.nn.sigmoid(got["fine"] + got["up"])
+        got["beyond"] = [
+            s[8 * o : 8 * o + 8] * weight_x + s[24 + 8 * o : 32 + 8 * o] * weight_xy
+            for o in range(3)
+        ]
+
+    def pool_of(q):
+        def task():
+            got["pool", q] = pool(q)
+
+        return task
+
+    def pooled_of(q):
+        return lambda: pooled(q, got["pool", q], got["ends"])
+
+    def fine_of(q):
+        def task():
+            got["fine", q] = fine(pair(q))
+
+        return task
+
+    low, high = slice(0, 256), slice(256, 512)
+
+    def low_coarse():
+        got["e", 0] = coarse(low)
+
+    def low_lift():
+        coarsened(low, got["e", 0])
+        got["q", 0], got["q", 1] = lift(section(0)), lift(section(1))
+
+    residual(0, [margins_pool, margins_pooled, margins_coarse, margins_coarsened, margins_lift])
+    first_level(pair(2))
+    finish_sections(0, 4)
+    residual(1, [margins_spread, margins_done])
+    first_level(pair(3))
+    finish_sections(1, 4)
+    residual(2, [pool_of(0), pooled_of(0), fine_of(0)])
+    finish_sections(2, 4)
+    residual(3, [pool_of(1), pooled_of(1), fine_of(1), low_coarse, low_lift])
+    finish_sections(3, 4)
+    pool_of(2)()
+    pool_of(3)()
+    got["up", 0] = spread(got["q", 0], table_ref[:, 0:256])
+    got["up", 1] = spread(got["q", 1], table_ref[:, 0:256])
+    pooled_of(2)()
+    got["e", 1] = coarse(section(2))
+    fine_of(2)()
+    pooled_of(3)()
+    coarsened(section(2), got["e", 1])
+    got["e", 1] = coarse(section(3))
+    fine_of(3)()
+    blend(0, got["fine", 0] + got["up", 0], got["beyond"])
+    coarsened(section(3), got["e", 1])
+    got["q", 2], got["q", 3] = lift(section(2)), lift(section(3))
+    blend(1, got["fine", 1] + got["up", 1], got["beyond"])
+    got["up", 2] = spread(got["q", 2], table_ref[:, 0:256])
+    got["up", 3] = spread(got["q", 3], table_ref[:, 0:256])
+    blend(2, got["fine", 2] + got["up", 2], got["beyond"])
+    blend(3, got["fine", 3] + got["up", 3], got["beyond"])
 
 
 def network(*made, **options):

time: 18.1 us -> 17.3 us (0.956)
  Pallas kernels: 17.9 us -> 17.1 us
    pallas_call x1, Pallas kernels: 6.09 us -> 5.36 us  [network(): pl.pallas_call(network_kernel, out_shape=jax.ShapeDtypeStruct((3, 8, 8, 1...]
where the time goes in v2:
time: 17.3 us; the launch traced here: 17.1 us
  Pallas kernels  17.1 us (99%)
    pallas_call x1, Pallas kernels, exchange(): pl.pallas_call(exchange_kernel, out_shape=(TAPS,) + MADE + (BLEND, TABLE)...  11.8 us
    pallas_call x1, Pallas kernels, network(): pl.pallas_call(network_kernel, out_shape=jax.ShapeDtypeStruct((3, 8, 8, 1...  5.36 us

profile of v2, /device:TPU:1, one launch (start us, length us, event | category | flops | bytes accessed | tf_op | source)
XLA Modules:
  0.0 17.1 jit_solution(6303665862870717276)
XLA Ops:
  0.0 11.8 %shard_map.136 = (bf16[96,1152]{1,0:T(8,128)(2,1)S(1)}, bf16[1280,128]{1,0:T(8,128)(2,1)S(1)}, bf16[672,256]{1,0:T(8,128)(2,1)S(1)}, bf16[656,256]{1,0:T(8,128)(...) custom-call(bf16[1,64,128]{2,1,0:T(8,128)(2,1)} %bitcast.9, ...), custom_call_target="tpu_custom_call" | custom-call | tf_op jit(solution)/shard_map/pallas_call | solution.py:567
  11.8 5.4 %shard_map.137 = f32[3,8,8,128]{3,2,1,0:T(8,128)} custom-call(bf16[96,1152]{1,0:T(8,128)(2,1)S(1)} %get-tuple-element.14.taps_ref, bf16[1280,128]{1,0:T(8,128)(2,1)S(1)} %get-tuple-element.15.conv_in_ref, bf16[672,256]{1,0:T(8,128)(2,1)S(1)} %get-tuple-element.16.conv_a_ref, bf16[656,256]{1,0:T(8,128)(2,1)S(1)} %get-tuple-element.17.conv_d_ref, ...), custom_call_target="tpu_custom_call" | custom-call | tf_op jit(solution)/shard_map/pallas_call | solution.py:853

commit v3 on v2

--- a/solution.py
+++ b/solution.py
@@ -156,7 +156,9 @@
         jnp.concatenate(stack, axis=0).astype(BF16),
         (((0,), (0,)), ((), ())),
         preferred_element_type=F32,
-    ).astype(BF16)
+    )
+    ones = within(iota((256, 640), 0), 92, 94) & (iota((256, 640), 1) % 128 == 80)
+    made = jnp.where(ones, 1.0, made).astype(BF16)
     for tile in range(5):
         conv_in_ref[256 * tile : 256 * tile + 256] = made[:, 128 * tile : 128 * tile + 128]
 
@@ -175,7 +177,18 @@
                 low = 96
             parts[n].append(jnp.where((lane >= low) & (lane < high), moved, 0.0))
     taps = jnp.concatenate([part for shift in parts for part in shift], axis=0).astype(BF16)
-    conv_a_ref[...] = dot(taps[:, 0:288], units_ref[...]).astype(BF16)
+    made = dot(taps[:, 0:288], units_ref[...])
+    rest = as_column(b_a_ref[...], 32)
+    lane = iota((32, 256), 1)
+    bias = jnp.zeros((32, 256), F32)
+    for n in range(3):
+        part = rest.astype(BF16).astype(F32)
+        bias = bias + jnp.where(lane == 92 + n, part, 0.0)
+        rest = rest - part
+    none = jnp.zeros((32, 256), F32)
+    once = jnp.concatenate([none, bias, none], axis=0)
+    none = jnp.concatenate([none] * 9, axis=0)
+    conv_a_ref[...] = (made + jnp.concatenate([none, once, once, once, once], axis=0)).astype(BF16)
 
     pad_ref[0:9] = jnp.zeros((9, 32, 128), BF16)
     pad_ref[0:9, 0:28, 0:36] = w_d_ref[...]
@@ -235,7 +248,7 @@
     block = jnp.where(row < 24, row % 8, jnp.where(within(row % 8, 3, 4), row % 8 + 5, row % 8))
     w_s_ref[...] = jnp.where(lane == block, w_o, 0.0).astype(BF16)
 
-    bias_ref[0:32] = jnp.broadcast_to(as_column(b_a_ref[...], 32), (32, 128))
+    bias_ref[0:32] = jnp.zeros((32, 128), F32)
     bias_ref[32:72] = jnp.broadcast_to(as_column(b_d_ref[...], 40), (40, 128))
     row = iota((48, 3), 0) % 24 // 8
     b_o = jnp.sum(jnp.where(row == iota((48, 3), 1), b_o_ref[...], 0.0), axis=1, keepdims=True)
@@ -523,7 +536,7 @@
         sent(send_edge_ref, 16)
 
 
-ROWS = (0, 1, 4, 8, 12, 5, 2, 9, 13, 3, 6, 7, 10, 14, 11, 15)
+ROWS = (0, 1, 4, 8, 12, 2, 3, 5, 9, 13, 6, 7, 10, 14, 11, 15)
 SOON = ROWS[:5]
 LATE = ROWS[5:]
 
@@ -603,7 +616,6 @@
     d_ref,
     e_ref,
 ):
-    bias_a = bias_ref[0:32]
     bias_d = jnp.concatenate([bias_ref[32:72]] * 8, axis=0)
     bias_o = bias_ref[72:120]
     weight_y, weight_x, weight_xy, scale = [blend_ref[8 * n : 8 * n + 8] for n in range(4)]
@@ -646,7 +658,7 @@
         block = (row + 1 if row < 12 else row - 6) if row != 12 else 6
         tile, nth = block // 3, block % 3
         centre = h_ref[tile, 32 * nth : 32 * nth + 32, at].astype(F32)
-        a_ref[places[row], :, at] = (centre + jnp.maximum(total + bias_a, 0.0)).astype(BF16)
+        a_ref[places[row], :, at] = (centre + jnp.maximum(total, 0.0)).astype(BF16)
 
     def pooled_rows(at):
         even = jnp.concatenate([a_ref[n, :, at] for n in (0, 2, 4, 6, 8, 12, 4, 11)], axis=0)
@@ -705,7 +717,12 @@
         own, other = parts
         q = jnp.concatenate([own[0:24] + own[24:48], other[0:24] + other[24:48]], axis=0)
         high = q.astype(BF16).astype(F32)
-        return dot(jnp.concatenate([high, q - high], axis=1).astype(BF16), table)
+        low = q - high
+        rows = [
+            jnp.concatenate([high[:, at : at + 128], low[:, at : at + 128]], axis=1)
+            for at in range(0, q.shape[1], 128)
+        ]
+        return dot(jnp.concatenate(rows, axis=0).astype(BF16), table)
 
     def fine(at):
         s = dot(w_s_ref[:, 0:320], a_ref[2:12, :, at].reshape(320, at.stop - at.start))
@@ -815,7 +832,7 @@
 
     def low_lift():
         coarsened(low, got["e", 0])
-        got["q", 0], got["q", 1] = lift(section(0)), lift(section(1))
+        got["q", 0] = lift(low)
 
     residual(0, [margins_pool, margins_pooled, margins_coarse, margins_coarsened, margins_lift])
     first_level(pair(2))
@@ -829,8 +846,8 @@
     finish_sections(3, 4)
     pool_of(2)()
     pool_of(3)()
-    got["up", 0] = spread(got["q", 0], table_ref[:, 0:256])
-    got["up", 1] = spread(got["q", 1], table_ref[:, 0:256])
+    up = spread(got["q", 0], table_ref[:, 0:256])
+    got["up", 0], got["up", 1] = up[0:48], up[48:96]
     pooled_of(2)()
     got["e", 1] = coarse(section(2))
     fine_of(2)()
@@ -840,10 +857,10 @@
     fine_of(3)()
     blend(0, got["fine", 0] + got["up", 0], got["beyond"])
     coarsened(section(3), got["e", 1])
-    got["q", 2], got["q", 3] = lift(section(2)), lift(section(3))
+    got["q", 1] = lift(high)
     blend(1, got["fine", 1] + got["up", 1], got["beyond"])
-    got["up", 2] = spread(got["q", 2], table_ref[:, 0:256])
-    got["up", 3] = spread(got["q", 3], table_ref[:, 0:256])
+    up = spread(got["q", 1], table_ref[:, 0:256])
+    got["up", 2], got["up", 3] = up[0:48], up[48:96]
     blend(2, got["fine", 2] + got["up", 2], got["beyond"])
     blend(3, got["fine", 3] + got["up", 3], got["beyond"])
 

time: 17.3 us -> 17.2 us (level)
  no operation moved by 1% of the time
where the time goes in v3:
time: 17.2 us; the launch traced here: 17.1 us
  Pallas kernels  17 us (99%)
    pallas_call x1, Pallas kernels, exchange(): pl.pallas_call(exchange_kernel, out_shape=(TAPS,) + MADE + (BLEND, TABLE)...  11.8 us
    pallas_call x1, Pallas kernels, network(): pl.pallas_call(network_kernel, out_shape=jax.ShapeDtypeStruct((3, 8, 8, 1...  5.28 us

profile of v3, /device:TPU:1, one launch (start us, length us, event | category | flops | bytes accessed | tf_op | source)
XLA Modules:
  0.0 17.1 jit_solution(4547474916132236091)
XLA Ops:
  0.0 11.8 %shard_map.136 = (bf16[96,1152]{1,0:T(8,128)(2,1)S(1)}, bf16[1280,128]{1,0:T(8,128)(2,1)S(1)}, bf16[672,256]{1,0:T(8,128)(2,1)S(1)}, bf16[656,256]{1,0:T(8,128)(...) custom-call(bf16[1,64,128]{2,1,0:T(8,128)(2,1)} %bitcast.9, ...), custom_call_target="tpu_custom_call" | custom-call | tf_op jit(solution)/shard_map/pallas_call | solution.py:580
  11.8 5.3 %shard_map.137 = f32[3,8,8,128]{3,2,1,0:T(8,128)} custom-call(bf16[96,1152]{1,0:T(8,128)(2,1)S(1)} %get-tuple-element.14.taps_ref, bf16[1280,128]{1,0:T(8,128)(2,1)S(1)} %get-tuple-element.15.conv_in_ref, bf16[672,256]{1,0:T(8,128)(2,1)S(1)} %get-tuple-element.16.conv_a_ref, bf16[656,256]{1,0:T(8,128)(2,1)S(1)} %get-tuple-element.17.conv_d_ref, ...), custom_call_target="tpu_custom_call" | custom-call | tf_op jit(solution)/shard_map/pallas_call | solution.py:870

commit v4 on v3

--- a/solution.py
+++ b/solution.py
@@ -385,20 +385,21 @@
     def _():
         pl.semaphore_signal(barrier, inc=1, device_id=mate, device_id_type=MESH)
 
-    for chip in range(4):
+    chips = [lax.rem(lax.div(gj, 2) + n, 4) for n in (2, 1, 3, 0)]
+    for chip in chips:
         for strip in (2 * gj, 2 * gj + 1):
             peer = (strip, 2 * chip + group)
             pl.semaphore_signal(barrier, inc=1, device_id=peer, device_id_type=MESH)
 
     @pl.when(gj > 0)
     def _():
-        for chip in range(4):
+        for chip in chips:
             peer = (2 * gj - 1, 2 * chip + group)
             pl.semaphore_signal(barrier, inc=1, device_id=peer, device_id_type=MESH)
 
     @pl.when(gj < 7)
     def _():
-        for chip in range(4):
+        for chip in chips:
             peer = (2 * gj + 2, 2 * chip + group)
             pl.semaphore_signal(barrier, inc=1, device_id=peer, device_id_type=MESH)
 
@@ -610,7 +611,9 @@
     bias_ref,
     blend_ref,
     table_ref,
+    out_hbm,
     out_ref,
+    out_sem,
     h_ref,
     a_ref,
     d_ref,
@@ -861,8 +864,16 @@
     blend(1, got["fine", 1] + got["up", 1], got["beyond"])
     up = spread(got["q", 1], table_ref[:, 0:256])
     got["up", 2], got["up", 3] = up[0:48], up[48:96]
+    def out(n):
+        part = (slice(None), slice(4 * n, 4 * n + 4))
+        return pltpu.make_async_copy(out_ref.at[part], out_hbm.at[part], out_sem.at[n])
+
+    out(0).start()
     blend(2, got["fine", 2] + got["up", 2], got["beyond"])
     blend(3, got["fine", 3] + got["up", 3], got["beyond"])
+    out(1).start()
+    out(0).wait()
+    out(1).wait()
 
 
 def network(*made, **options):
@@ -871,8 +882,10 @@
         network_kernel,
         out_shape=jax.ShapeDtypeStruct((3, 8, 8, 128), F32),
         in_specs=[vmem] * 9,
-        out_specs=vmem,
+        out_specs=pl.BlockSpec(memory_space=pl.ANY),
         scratch_shapes=[
+            pltpu.VMEM((3, 8, 8, 128), F32),
+            pltpu.SemaphoreType.DMA((2,)),
             pltpu.VMEM((5, 256, 1152), BF16),
             pltpu.VMEM((14, 32, 1152), BF16),
             pltpu.VMEM((8, 3, 32, 640), BF16),

time: 17.2 us -> 17.2 us (level)
  no operation moved by 1% of the time
where the time goes in v4:
time: 17.2 us; the launch traced here: 17 us
  Pallas kernels  17 us (99%)
    pallas_call x1, Pallas kernels, exchange(): pl.pallas_call(exchange_kernel, out_shape=(TAPS,) + MADE + (BLEND, TABLE)...  11.8 us
    pallas_call x1, Pallas kernels, network(): pl.pallas_call(network_kernel, out_shape=jax.ShapeDtypeStruct((3, 8, 8, 1...  5.28 us

profile of v4, /device:TPU:1, one launch (start us, length us, event | category | flops | bytes accessed | tf_op | source)
XLA Modules:
  0.0 17.0 jit_solution(1331482356076044486)
XLA Ops:
  0.0 11.8 %shard_map.136 = (bf16[96,1152]{1,0:T(8,128)(2,1)S(1)}, bf16[1280,128]{1,0:T(8,128)(2,1)S(1)}, bf16[672,256]{1,0:T(8,128)(2,1)S(1)}, bf16[656,256]{1,0:T(8,128)(...) custom-call(bf16[1,64,128]{2,1,0:T(8,128)(2,1)} %bitcast.9, ...), custom_call_target="tpu_custom_call" | custom-call | tf_op jit(solution)/shard_map/pallas_call | solution.py:581
  11.8 5.3 %shard_map.137 = f32[3,8,8,128]{3,2,1,0:T(8,128)} custom-call(bf16[96,1152]{1,0:T(8,128)(2,1)S(1)} %get-tuple-element.14.taps_ref, bf16[1280,128]{1,0:T(8,128)(2,1)S(1)} %get-tuple-element.15.conv_in_ref, bf16[672,256]{1,0:T(8,128)(2,1)S(1)} %get-tuple-element.16.conv_a_ref, bf16[656,256]{1,0:T(8,128)(2,1)S(1)} %get-tuple-element.17.conv_d_ref, ...), custom_call_target="tpu_custom_call" | custom-call | tf_op jit(solution)/shard_map/pallas_call | solution.py:881

commit v5 on v4

--- a/solution.py
+++ b/solution.py
@@ -459,12 +459,18 @@
                     device_id_type=MESH,
                 ).start()
 
-            @pl.when(here & wanted)
-            def _():
-                pltpu.make_async_copy(source, target, recv_sem.at[kind]).start()
-
     for row in SOON:
         send(row)
+
+    @pl.when(gj == column)
+    def _():
+        pltpu.make_async_copy(send_ref.at[gi], got_ref.at[odd, gj], recv_sem.at[0]).start()
+
+    @pl.when(inner & (gj == beside))
+    def _():
+        pltpu.make_async_copy(
+            send_edge_ref.at[gi], got_edge_ref.at[1 - odd, gj], recv_sem.at[1]
+        ).start()
 
     for load in loads[1:]:
         load.wait()

time: 17.2 us -> 17.2 us (level)
  no operation moved by 1% of the time
where the time goes in v5:
time: 17.2 us; the launch traced here: 17 us
  Pallas kernels  17 us (99%)
    pallas_call x1, Pallas kernels, exchange(): pl.pallas_call(exchange_kernel, out_shape=(TAPS,) + MADE + (BLEND, TABLE)...  11.8 us
    pallas_call x1, Pallas kernels, network(): pl.pallas_call(network_kernel, out_shape=jax.ShapeDtypeStruct((3, 8, 8, 1...  5.27 us

profile of v5, /device:TPU:1, one launch (start us, length us, event | category | flops | bytes accessed | tf_op | source)
XLA Modules:
  0.0 17.0 jit_solution(7198630841888062061)
XLA Ops:
  0.0 11.8 %shard_map.136 = (bf16[96,1152]{1,0:T(8,128)(2,1)S(1)}, bf16[1280,128]{1,0:T(8,128)(2,1)S(1)}, bf16[672,256]{1,0:T(8,128)(2,1)S(1)}, bf16[656,256]{1,0:T(8,128)(...) custom-call(bf16[1,64,128]{2,1,0:T(8,128)(2,1)} %bitcast.9, ...), custom_call_target="tpu_custom_call" | custom-call | tf_op jit(solution)/shard_map/pallas_call | solution.py:587
  11.8 5.3 %shard_map.137 = f32[3,8,8,128]{3,2,1,0:T(8,128)} custom-call(bf16[96,1152]{1,0:T(8,128)(2,1)S(1)} %get-tuple-element.14.taps_ref, bf16[1280,128]{1,0:T(8,128)(2,1)S(1)} %get-tuple-element.15.conv_in_ref, bf16[672,256]{1,0:T(8,128)(2,1)S(1)} %get-tuple-element.16.conv_a_ref, bf16[656,256]{1,0:T(8,128)(2,1)S(1)} %get-tuple-element.17.conv_d_ref, ...), custom_call_target="tpu_custom_call" | custom-call | tf_op jit(solution)/shard_map/pallas_call | solution.py:887

commit v6 on v5

--- a/solution.py
+++ b/solution.py
@@ -751,19 +751,34 @@
     sums = {}
     along = iota((32, 128), 1)
 
-    def finish_margins(tile):
-        for row in tiles[tile][2]:
+    def add(row, part):
+        sums[row] = sums[row] + part if row in sums else part
+
+    def margin_products(first, count, *places):
+        h = jnp.concatenate([h_ref[tile, :, margins] for tile, _, _ in places], axis=1)
+        product = dot(conv_a_ref[96 * first : 96 * (first + count)], h)
+        product = product.reshape(count, 3, 32, h.shape[1])
+        for half, (tile, skip, rows) in enumerate(places):
+            for n, row in enumerate(rows):
+                part = product[skip + n, :, :, 128 * half : 128 * half + 128]
+                add(row, part)
+                if tile == 1 and row == 5:
+                    add(12, part)
+
+    def finish_margins(rows):
+        for row in rows:
             before, here, after = sums[row][0], sums[row][1], sums[row][2]
             before = jnp.where(along >= 16, pltpu.roll(before, 16, 1), 0.0)
             after = jnp.where(along < 112, pltpu.roll(after, 112, 1), 0.0)
             finish(row, margins, here + before + after)
 
-    for tile in range(5):
-        products(tile, margins, sums)
-        if tile > 0:
-            finish_margins(tile - 1)
+    margin_products(1, 5, (1, 0, tiles[1][1]), (3, 0, tiles[3][1]))
+    finish_margins((3, 9))
+    margin_products(0, 7, (2, 0, tiles[2][1]), (0, 3, tiles[0][1]))
+    finish_margins((0, 1, 2, 4, 5, 6, 7, 8, 12, 13))
+    margin_products(1, 2, (4, 0, tiles[4][1]))
     first_level(pair(1))
-    finish_margins(4)
+    finish_margins((10, 11))
 
     p = [{}, {}, {}, {}]
 

time: 17.2 us -> 17.3 us (level)
  no operation moved by 1% of the time
where the time goes in v6:
time: 17.3 us; the launch traced here: 17.1 us
  Pallas kernels  17.1 us (99%)
    pallas_call x1, Pallas kernels, exchange(): pl.pallas_call(exchange_kernel, out_shape=(TAPS,) + MADE + (BLEND, TABLE)...  11.8 us
    pallas_call x1, Pallas kernels, network(): pl.pallas_call(network_kernel, out_shape=jax.ShapeDtypeStruct((3, 8, 8, 1...  5.34 us

profile of v6, /device:TPU:1, one launch (start us, length us, event | category | flops | bytes accessed | tf_op | source)
XLA Modules:
  0.0 17.1 jit_solution(2382302790822562758)
XLA Ops:
  0.0 11.8 %shard_map.136 = (bf16[96,1152]{1,0:T(8,128)(2,1)S(1)}, bf16[1280,128]{1,0:T(8,128)(2,1)S(1)}, bf16[672,256]{1,0:T(8,128)(2,1)S(1)}, bf16[656,256]{1,0:T(8,128)(...) custom-call(bf16[1,64,128]{2,1,0:T(8,128)(2,1)} %bitcast.9, ...), custom_call_target="tpu_custom_call" | custom-call | tf_op jit(solution)/shard_map/pallas_call | solution.py:587
  11.8 5.3 %shard_map.137 = f32[3,8,8,128]{3,2,1,0:T(8,128)} custom-call(bf16[96,1152]{1,0:T(8,128)(2,1)S(1)} %get-tuple-element.14.taps_ref, bf16[1280,128]{1,0:T(8,128)(2,1)S(1)} %get-tuple-element.15.conv_in_ref, bf16[672,256]{1,0:T(8,128)(2,1)S(1)} %get-tuple-element.16.conv_a_ref, bf16[656,256]{1,0:T(8,128)(2,1)S(1)} %get-tuple-element.17.conv_d_ref, ...), custom_call_target="tpu_custom_call" | custom-call | tf_op jit(solution)/shard_map/pallas_call | solution.py:902
